TPU v7x, 256 devices: a whole 4x4x8 slice. The times are simulated.
256 devices in a mesh: gx: 8 (over y, x_lo), gy: 32 (over x_hi, z, core).
Axes of the slice: x: 4 (x_hi: 2, x_lo: 2; x = x_hi * 2 + x_lo), y: 4, z: 8, core: 2. Of those that a mesh axis runs over, the one named last changes fastest.
Arguments:
- pressure: float32 [28, 1024, 1024], P(None, 'gy', 'gx'), may hold values from -6 to 6
- previous: float32 [28, 1024, 1024], P(None, 'gy', 'gx'), may hold values from -6 to 6
- branch_state: float32 [28, 1024, 1024], P(None, 'gy', 'gx'), may hold values from -6 to 6
- wall_mask: int32 [28, 1024, 1024], P(None, 'gy', 'gx'), may hold values 0 or 1
- material: int32 [28, 1024, 1024], P(None, 'gy', 'gx'), may hold values from 0 to 7
- ghost_low: float32 [1024, 1024], P('gy', 'gx'), may hold values from -6 to 6
- ghost_high: float32 [1024, 1024], P('gy', 'gx'), may hold values from -6 to 6
- wall_table: float32 [4, 8], replicated, may hold values from 0.05 to 3, as said below
Outputs:
- final_pressure: float32 [28, 1024, 1024], P(None, 'gy', 'gx')
- final_state: float32 [28, 1024, 1024], P(None, 'gy', 'gx')
Inputs may be any that keep to these rules, and one draw needn't show every extreme that they name: `wall_table`: row 0 lies in 0.05 to 3, rows 1 to 3 in 0.05 to 1.
All inputs are finite; a program needn't handle non-finite values. No bound on the sum of `wall_mask` on one device may be relied on, other than what follows from the above.
Results may differ from a plain program's by a relative error of at most 0.00002.
Values sent between devices are 32-bit elements; how exact they have to be, the bound alone decides.
A program may use at most 64 MiB of HBM per device.

v0:
```python
import jax
import jax.numpy as jnp
from jax import lax
from jax.sharding import PartitionSpec as P

ITERS = 8


courant_sq = 0.33


def padded(cells, sides, width):
    for axis, dim in sides:
        count = lax.axis_size(axis)
        ends = count - 1
        head = lax.slice_in_dim(cells, 0, width, axis=dim)
        tail = lax.slice_in_dim(cells, cells.shape[dim] - width, cells.shape[dim], axis=dim)
        cells = jnp.concatenate(
            [
                lax.ppermute(tail, axis, [(i, (i + 1) % count) for i in range(ends)]),
                cells,
                lax.ppermute(head, axis, [((i + 1) % count, i) for i in range(ends)]),
            ],
            axis=dim,
        )
    return cells


def laplace(field, side_y, side_x, low, high):
    below = jnp.concatenate([low[None], field[:-1]], axis=0)
    above = jnp.concatenate([field[1:], high[None]], axis=0)
    return (
        side_y[:, 2:]
        + side_y[:, :-2]
        + (side_x[:, :, 2:] + side_x[:, :, :-2])
        + (below + above)
        - 6.0 * field
    )


def wall_terms(wall_mask, material, wall_table):
    maskf = wall_mask.astype(jnp.float32)
    picks = []
    for row in range(4):
        total = jnp.zeros(material.shape, jnp.float32)
        for index in range(wall_table.shape[1]):
            total = total + jnp.where(material == index, wall_table[row, index], 0.0)
        picks.append(total)
    return (picks[0] * maskf, picks[1] * maskf, picks[2], picks[3], wall_mask == 1)


def update(field, older, state, lapl, terms):
    beta, weight, decay, couple, walls = terms
    source = 2.0 * field - older + courant_sq * lapl
    newer = (source + beta * older - weight * state) / (1.0 + beta)
    state = jnp.where(walls, decay * state + couple * (newer - older), state)
    return (newer, state)


def body(pressure, previous, branch_state, wall_mask, material, ghost_low, ghost_high, wall_table):
    terms = wall_terms(wall_mask, material, wall_table)
    field, older, state = (pressure, previous, branch_state)
    for step in range(ITERS):
        framed = padded(field, (("gx", 2), ("gy", 1)), 1)
        side_y = framed[:, :, 1:-1]
        side_x = framed[:, 1:-1, :]
        lapl = laplace(field, side_y, side_x, ghost_low, ghost_high)
        newer, state = update(field, older, state, lapl, terms)
        older, field = (field, newer)
    return (field, state)


def solution(mesh):
    return jax.shard_map(
        body,
        mesh=mesh,
        in_specs=(
            P(None, "gy", "gx"),
            P(None, "gy", "gx"),
            P(None, "gy", "gx"),
            P(None, "gy", "gx"),
            P(None, "gy", "gx"),
            P("gy", "gx"),
            P("gy", "gx"),
            P(),
        ),
        out_specs=(P(None, "gy", "gx"), P(None, "gy", "gx")),
        check_vma=False,
    )
```

profile of v0, /device:TPU:22, one launch (start us, length us, event | category | flops | bytes accessed | tf_op | source)
XLA Modules:
  0.0 280.5 jit_solution(12350090179718529915)
XLA Ops:
  10.2 8.0 %collective-permute-done.1 = f32[28,32,1]{2,1,0:T(8,128)S(1)} collective-permute-done((f32[28,32,1]{2,1,0:T(8,128)S(1)}, f32[28,32,1]{2,1,0:T(8,128)S(1)}, u32[]{:S(2)}, u32[]{:S(2)}) %collective-permute-start.1) | collective-permute-done | bytes 3616 | tf_op jit(solution)/shard_map/ppermute | solution.py:22
  18.2 7.7 %collective-permute-done = f32[28,32,1]{2,1,0:T(8,128)S(1)} collective-permute-done((f32[28,32,1]{2,1,0:T(8,128)S(1)}, f32[28,32,1]{2,1,0:T(8,128)S(1)}, u32[]{:S(2)}, u32[]{:S(2)}) %collective-permute-start) | collective-permute-done | bytes 3616 | tf_op jit(solution)/shard_map/ppermute | solution.py:20
  26.2 7.2 %collective-permute-start.2 = (f32[28,1,130]{2,1,0:T(1,128)S(1)}, f32[28,1,130]{2,1,0:T(1,128)S(1)}, u32[]{:S(2)}, u32[]{:S(2)}) collective-permute-start(f32[28,1,130]{2,1,0:T(1,128)S(1)} %get-tuple-element.37), channel_id=1, source_target_pairs={{1,0},{2,1},{3,2},{4,3},{5,4},{6,5},{7,6},{8,7},{9,8},{10,9},{11,1... | collective-permute-start | bytes 43688 | tf_op jit(solution)/shard_map/ppermute | solution.py:22
  36.0 6.2 %collective-permute-done.3 = f32[28,1,130]{2,1,0:T(1,128)S(1)} collective-permute-done((f32[28,1,130]{2,1,0:T(1,128)S(1)}, f32[28,1,130]{2,1,0:T(1,128)S(1)}, u32[]{:S(2)}, u32[]{:S(2)}) %collective-permute-start.3) | collective-permute-done | bytes 14592 | tf_op jit(solution)/shard_map/ppermute | solution.py:20
  42.9 11.5 %fusion.7 = (f32[28,32,128]{2,1,0:T(8,128)S(1)}, f32[28,32,128]{2,1,0:T(8,128)S(1)}, f32[28,32,128]{2,1,0:T(8,128)S(1)}, pred[28,32,128]{2,1,0:T(8,128)(4,1)S(1)...) fusion(f32[1,32,128]{2,1,0:T(8,128)S(1)} %bitcast.34, ...), kind=kLoop, calls=%fused_computation.23 | loop fusion | flops 7798784 | bytes 5541376 | tf_op jit(solution)/shard_map/div | solution.py:55
  61.3 7.7 %collective-permute-done.5 = f32[28,32,1]{2,1,0:T(8,128)S(1)} collective-permute-done((f32[28,32,1]{2,1,0:T(8,128)S(1)}, f32[28,32,1]{2,1,0:T(8,128)S(1)}, u32[]{:S(2)}, u32[]{:S(2)}) %collective-permute-start.5) | collective-permute-done | bytes 3616 | tf_op jit(solution)/shard_map/ppermute | solution.py:22
  73.1 5.8 %collective-permute-start.6 = (f32[28,1,130]{2,1,0:T(1,128)S(1)}, f32[28,1,130]{2,1,0:T(1,128)S(1)}, u32[]{:S(2)}, u32[]{:S(2)}) collective-permute-start(f32[28,1,130]{2,1,0:T(1,128)S(1)} %get-tuple-element.35), channel_id=1, source_target_pairs={{1,0},{2,1},{3,2},{4,3},{5,4},{6,5},{7,6},{8,7},{9,8},{10,9},{11,1... | collective-permute-start | bytes 43688 | tf_op jit(solution)/shard_map/ppermute | solution.py:22
  81.0 6.8 %collective-permute-done.7 = f32[28,1,130]{2,1,0:T(1,128)S(1)} collective-permute-done((f32[28,1,130]{2,1,0:T(1,128)S(1)}, f32[28,1,130]{2,1,0:T(1,128)S(1)}, u32[]{:S(2)}, u32[]{:S(2)}) %collective-permute-start.7) | collective-permute-done | bytes 14592 | tf_op jit(solution)/shard_map/ppermute | solution.py:20
  87.8 11.6 %fusion.15 = (f32[28,32,128]{2,1,0:T(8,128)S(1)}, f32[28,32,128]{2,1,0:T(8,128)S(1)}, f32[28,32,128]{2,1,0:T(8,128)S(1)}, pred[28,32,128]{2,1,0:T(8,128)(4,1)S(1)}) fusion(f32[1,32,128]{2,1,0:T(8,128)S(1)} %bitcast.35, f32[1,32,128]{2,1,0:T(8,128)S(1)} %bitcast.43, f32[28,32,128]{2,1,0:T(8,128)S(1)} %get-tuple-element.12, ...), kind=kLoop, calls=%fused_computation.31 | loop fusion | flops 7225344 | bytes 6573568 | tf_op jit(solution)/shard_map/div | solution.py:55
  106.3 7.7 %collective-permute-done.9 = f32[28,32,1]{2,1,0:T(8,128)S(1)} collective-permute-done((f32[28,32,1]{2,1,0:T(8,128)S(1)}, f32[28,32,1]{2,1,0:T(8,128)S(1)}, u32[]{:S(2)}, u32[]{:S(2)}) %collective-permute-start.9) | collective-permute-done | bytes 3616 | tf_op jit(solution)/shard_map/ppermute | solution.py:22
  122.7 6.9 %collective-permute-done.11 = f32[28,1,130]{2,1,0:T(1,128)S(1)} collective-permute-done((f32[28,1,130]{2,1,0:T(1,128)S(1)}, f32[28,1,130]{2,1,0:T(1,128)S(1)}, u32[]{:S(2)}, u32[]{:S(2)}) %collective-permute-start.11) | collective-permute-done | bytes 14592 | tf_op jit(solution)/shard_map/ppermute | solution.py:20
  137.7 7.6 %collective-permute-done.13 = f32[28,32,1]{2,1,0:T(8,128)S(1)} collective-permute-done((f32[28,32,1]{2,1,0:T(8,128)S(1)}, f32[28,32,1]{2,1,0:T(8,128)S(1)}, u32[]{:S(2)}, u32[]{:S(2)}) %collective-permute-start.13) | collective-permute-done | bytes 3616 | tf_op jit(solution)/shard_map/ppermute | solution.py:22
  152.2 6.9 %collective-permute-done.15 = f32[28,1,130]{2,1,0:T(1,128)S(1)} collective-permute-done((f32[28,1,130]{2,1,0:T(1,128)S(1)}, f32[28,1,130]{2,1,0:T(1,128)S(1)}, u32[]{:S(2)}, u32[]{:S(2)}) %collective-permute-start.15) | collective-permute-done | bytes 14592 | tf_op jit(solution)/shard_map/ppermute | solution.py:20
  167.1 7.9 %collective-permute-done.17 = f32[28,32,1]{2,1,0:T(8,128)S(1)} collective-permute-done((f32[28,32,1]{2,1,0:T(8,128)S(1)}, f32[28,32,1]{2,1,0:T(8,128)S(1)}, u32[]{:S(2)}, u32[]{:S(2)}) %collective-permute-start.17) | collective-permute-done | bytes 3616 | tf_op jit(solution)/shard_map/ppermute | solution.py:22
  181.3 6.8 %collective-permute-done.19 = f32[28,1,130]{2,1,0:T(1,128)S(1)} collective-permute-done((f32[28,1,130]{2,1,0:T(1,128)S(1)}, f32[28,1,130]{2,1,0:T(1,128)S(1)}, u32[]{:S(2)}, u32[]{:S(2)}) %collective-permute-start.19) | collective-permute-done | bytes 14592 | tf_op jit(solution)/shard_map/ppermute | solution.py:20
  191.3 4.8 %collective-permute-start.20 = (f32[28,32,1]{2,1,0:T(8,128)S(1)}, f32[28,32,1]{2,1,0:T(8,128)S(1)}, u32[]{:S(2)}, u32[]{:S(2)}) collective-permute-start(f32[28,32,1]{2,1,0:T(8,128)S(1)} %get-tuple-element.50), channel_id=1, source_target_pairs={{0,32},{32,64},{64,96},{96,128},{128,160},{160,192},{192,224},{1,3... | collective-permute-start | bytes 10760 | tf_op jit(solution)/shard_map/ppermute | solution.py:20
  196.1 8.3 %collective-permute-done.21 = f32[28,32,1]{2,1,0:T(8,128)S(1)} collective-permute-done((f32[28,32,1]{2,1,0:T(8,128)S(1)}, f32[28,32,1]{2,1,0:T(8,128)S(1)}, u32[]{:S(2)}, u32[]{:S(2)}) %collective-permute-start.21) | collective-permute-done | bytes 3616 | tf_op jit(solution)/shard_map/ppermute | solution.py:22
  210.6 6.5 %collective-permute-done.23 = f32[28,1,130]{2,1,0:T(1,128)S(1)} collective-permute-done((f32[28,1,130]{2,1,0:T(1,128)S(1)}, f32[28,1,130]{2,1,0:T(1,128)S(1)}, u32[]{:S(2)}, u32[]{:S(2)}) %collective-permute-start.23) | collective-permute-done | bytes 14592 | tf_op jit(solution)/shard_map/ppermute | solution.py:20
  220.2 5.0 %collective-permute-start.24 = (f32[28,32,1]{2,1,0:T(8,128)S(1)}, f32[28,32,1]{2,1,0:T(8,128)S(1)}, u32[]{:S(2)}, u32[]{:S(2)}) collective-permute-start(f32[28,32,1]{2,1,0:T(8,128)S(1)} %get-tuple-element.46), channel_id=1, source_target_pairs={{0,32},{32,64},{64,96},{96,128},{128,160},{160,192},{192,224},{1,3... | collective-permute-start | bytes 10760 | tf_op jit(solution)/shard_map/ppermute | solution.py:20
  225.2 9.5 %collective-permute-done.25 = f32[28,32,1]{2,1,0:T(8,128)S(1)} collective-permute-done((f32[28,32,1]{2,1,0:T(8,128)S(1)}, f32[28,32,1]{2,1,0:T(8,128)S(1)}, u32[]{:S(2)}, u32[]{:S(2)}) %collective-permute-start.25) | collective-permute-done | bytes 3616 | tf_op jit(solution)/shard_map/ppermute | solution.py:22
  240.9 6.4 %collective-permute-done.27 = f32[28,1,130]{2,1,0:T(1,128)S(1)} collective-permute-done((f32[28,1,130]{2,1,0:T(1,128)S(1)}, f32[28,1,130]{2,1,0:T(1,128)S(1)}, u32[]{:S(2)}, u32[]{:S(2)}) %collective-permute-start.27) | collective-permute-done | bytes 14592 | tf_op jit(solution)/shard_map/ppermute | solution.py:20
  250.5 5.2 %collective-permute-start.28 = (f32[28,32,1]{2,1,0:T(8,128)S(1)}, f32[28,32,1]{2,1,0:T(8,128)S(1)}, u32[]{:S(2)}, u32[]{:S(2)}) collective-permute-start(f32[28,32,1]{2,1,0:T(8,128)S(1)} %get-tuple-element.40), channel_id=1, source_target_pairs={{0,32},{32,64},{64,96},{96,128},{128,160},{160,192},{192,224},{1,3... | collective-permute-start | bytes 10760 | tf_op jit(solution)/shard_map/ppermute | solution.py:20
  255.7 9.5 %collective-permute-done.29 = f32[28,32,1]{2,1,0:T(8,128)S(1)} collective-permute-done((f32[28,32,1]{2,1,0:T(8,128)S(1)}, f32[28,32,1]{2,1,0:T(8,128)S(1)}, u32[]{:S(2)}, u32[]{:S(2)}) %collective-permute-start.29) | collective-permute-done | bytes 3616 | tf_op jit(solution)/shard_map/ppermute | solution.py:22
  272.2 6.3 %collective-permute-done.31 = f32[28,1,130]{2,1,0:T(1,128)S(1)} collective-permute-done((f32[28,1,130]{2,1,0:T(1,128)S(1)}, f32[28,1,130]{2,1,0:T(1,128)S(1)}, u32[]{:S(2)}, u32[]{:S(2)}) %collective-permute-start.31) | collective-permute-done | bytes 14592 | tf_op jit(solution)/shard_map/ppermute | solution.py:20
  (90 shorter events, 101.8 us)
Async XLA Ops:
  2.0 16.2 %collective-permute-start.1 = (f32[28,32,1]{2,1,0:T(8,128)S(1)}, f32[28,32,1]{2,1,0:T(8,128)S(1)}, u32[]{:S(2)}, u32[]{:S(2)}) collective-permute-start(f32[28,32,1]{2,1,0:T(8,128)S(1)} %get-tuple-element.69), channel_id=1, source_target_pairs={{32,0},{64,32},{96,64},{128,96},{160,128},{192,160},{224,192},{33,... | collective-permute-start | bytes 10760 | tf_op jit(solution)/shard_map/ppermute | solution.py:22
  4.8 21.1 %collective-permute-start = (f32[28,32,1]{2,1,0:T(8,128)S(1)}, f32[28,32,1]{2,1,0:T(8,128)S(1)}, u32[]{:S(2)}, u32[]{:S(2)}) collective-permute-start(f32[28,32,1]{2,1,0:T(8,128)S(1)} %get-tuple-element.70), channel_id=1, source_target_pairs={{0,32},{32,64},{64,96},{96,128},{128,160},{160,192},{192,224},{1,3... | collective-permute-start | bytes 10760 | tf_op jit(solution)/shard_map/ppermute | solution.py:20
  26.2 9.8 %collective-permute-start.2 = (f32[28,1,130]{2,1,0:T(1,128)S(1)}, f32[28,1,130]{2,1,0:T(1,128)S(1)}, u32[]{:S(2)}, u32[]{:S(2)}) collective-permute-start(f32[28,1,130]{2,1,0:T(1,128)S(1)} %get-tuple-element.37), channel_id=1, source_target_pairs={{1,0},{2,1},{3,2},{4,3},{5,4},{6,5},{7,6},{8,7},{9,8},{10,9},{11,1... | collective-permute-start | bytes 43688 | tf_op jit(solution)/shard_map/ppermute | solution.py:22
  33.3 8.8 %collective-permute-start.3 = (f32[28,1,130]{2,1,0:T(1,128)S(1)}, f32[28,1,130]{2,1,0:T(1,128)S(1)}, u32[]{:S(2)}, u32[]{:S(2)}) collective-permute-start(f32[28,1,130]{2,1,0:T(1,128)S(1)} %get-tuple-element.38), channel_id=1, source_target_pairs={{0,1},{1,2},{2,3},{3,4},{4,5},{5,6},{6,7},{7,8},{8,9},{9,10},{10,1... | collective-permute-start | bytes 43688 | tf_op jit(solution)/shard_map/ppermute | solution.py:20
  54.5 14.4 %collective-permute-start.5 = (f32[28,32,1]{2,1,0:T(8,128)S(1)}, f32[28,32,1]{2,1,0:T(8,128)S(1)}, u32[]{:S(2)}, u32[]{:S(2)}) collective-permute-start(f32[28,32,1]{2,1,0:T(8,128)S(1)} %get-tuple-element.65), channel_id=1, source_target_pairs={{32,0},{64,32},{96,64},{128,96},{160,128},{192,160},{224,192},{33,... | collective-permute-start | bytes 10760 | tf_op jit(solution)/shard_map/ppermute | solution.py:22
  56.5 16.4 %collective-permute-start.4 = (f32[28,32,1]{2,1,0:T(8,128)S(1)}, f32[28,32,1]{2,1,0:T(8,128)S(1)}, u32[]{:S(2)}, u32[]{:S(2)}) collective-permute-start(f32[28,32,1]{2,1,0:T(8,128)S(1)} %get-tuple-element.66), channel_id=1, source_target_pairs={{0,32},{32,64},{64,96},{96,128},{128,160},{160,192},{192,224},{1,3... | collective-permute-start | bytes 10760 | tf_op jit(solution)/shard_map/ppermute | solution.py:20
  79.0 8.8 %collective-permute-start.7 = (f32[28,1,130]{2,1,0:T(1,128)S(1)}, f32[28,1,130]{2,1,0:T(1,128)S(1)}, u32[]{:S(2)}, u32[]{:S(2)}) collective-permute-start(f32[28,1,130]{2,1,0:T(1,128)S(1)} %get-tuple-element.36), channel_id=1, source_target_pairs={{0,1},{1,2},{2,3},{3,4},{4,5},{5,6},{6,7},{7,8},{8,9},{9,10},{10,1... | collective-permute-start | bytes 43688 | tf_op jit(solution)/shard_map/ppermute | solution.py:20
  99.6 14.4 %collective-permute-start.9 = (f32[28,32,1]{2,1,0:T(8,128)S(1)}, f32[28,32,1]{2,1,0:T(8,128)S(1)}, u32[]{:S(2)}, u32[]{:S(2)}) collective-permute-start(f32[28,32,1]{2,1,0:T(8,128)S(1)} %get-tuple-element.61), channel_id=1, source_target_pairs={{32,0},{64,32},{96,64},{128,96},{160,128},{192,160},{224,192},{33,... | collective-permute-start | bytes 10760 | tf_op jit(solution)/shard_map/ppermute | solution.py:22
  101.5 15.0 %collective-permute-start.8 = (f32[28,32,1]{2,1,0:T(8,128)S(1)}, f32[28,32,1]{2,1,0:T(8,128)S(1)}, u32[]{:S(2)}, u32[]{:S(2)}) collective-permute-start(f32[28,32,1]{2,1,0:T(8,128)S(1)} %get-tuple-element.62), channel_id=1, source_target_pairs={{0,32},{32,64},{64,96},{96,128},{128,160},{160,192},{192,224},{1,3... | collective-permute-start | bytes 10760 | tf_op jit(solution)/shard_map/ppermute | solution.py:20
  120.7 8.9 %collective-permute-start.11 = (f32[28,1,130]{2,1,0:T(1,128)S(1)}, f32[28,1,130]{2,1,0:T(1,128)S(1)}, u32[]{:S(2)}, u32[]{:S(2)}) collective-permute-start(f32[28,1,130]{2,1,0:T(1,128)S(1)} %get-tuple-element.34), channel_id=1, source_target_pairs={{0,1},{1,2},{2,3},{3,4},{4,5},{5,6},{6,7},{7,8},{8,9},{9,10},{10,1... | collective-permute-start | bytes 43688 | tf_op jit(solution)/shard_map/ppermute | solution.py:20
  130.9 14.3 %collective-permute-start.13 = (f32[28,32,1]{2,1,0:T(8,128)S(1)}, f32[28,32,1]{2,1,0:T(8,128)S(1)}, u32[]{:S(2)}, u32[]{:S(2)}) collective-permute-start(f32[28,32,1]{2,1,0:T(8,128)S(1)} %get-tuple-element.57), channel_id=1, source_target_pairs={{32,0},{64,32},{96,64},{128,96},{160,128},{192,160},{224,192},{33,... | collective-permute-start | bytes 10760 | tf_op jit(solution)/shard_map/ppermute | solution.py:22
  132.8 14.2 %collective-permute-start.12 = (f32[28,32,1]{2,1,0:T(8,128)S(1)}, f32[28,32,1]{2,1,0:T(8,128)S(1)}, u32[]{:S(2)}, u32[]{:S(2)}) collective-permute-start(f32[28,32,1]{2,1,0:T(8,128)S(1)} %get-tuple-element.58), channel_id=1, source_target_pairs={{0,32},{32,64},{64,96},{96,128},{128,160},{160,192},{192,224},{1,3... | collective-permute-start | bytes 10760 | tf_op jit(solution)/shard_map/ppermute | solution.py:20
  150.1 8.9 %collective-permute-start.15 = (f32[28,1,130]{2,1,0:T(1,128)S(1)}, f32[28,1,130]{2,1,0:T(1,128)S(1)}, u32[]{:S(2)}, u32[]{:S(2)}) collective-permute-start(f32[28,1,130]{2,1,0:T(1,128)S(1)} %get-tuple-element.32), channel_id=1, source_target_pairs={{0,1},{1,2},{2,3},{3,4},{4,5},{5,6},{6,7},{7,8},{8,9},{9,10},{10,1... | collective-permute-start | bytes 43688 | tf_op jit(solution)/shard_map/ppermute | solution.py:20
  160.3 14.7 %collective-permute-start.17 = (f32[28,32,1]{2,1,0:T(8,128)S(1)}, f32[28,32,1]{2,1,0:T(8,128)S(1)}, u32[]{:S(2)}, u32[]{:S(2)}) collective-permute-start(f32[28,32,1]{2,1,0:T(8,128)S(1)} %get-tuple-element.53), channel_id=1, source_target_pairs={{32,0},{64,32},{96,64},{128,96},{160,128},{192,160},{224,192},{33,... | collective-permute-start | bytes 10760 | tf_op jit(solution)/shard_map/ppermute | solution.py:22
  162.3 14.3 %collective-permute-start.16 = (f32[28,32,1]{2,1,0:T(8,128)S(1)}, f32[28,32,1]{2,1,0:T(8,128)S(1)}, u32[]{:S(2)}, u32[]{:S(2)}) collective-permute-start(f32[28,32,1]{2,1,0:T(8,128)S(1)} %get-tuple-element.54), channel_id=1, source_target_pairs={{0,32},{32,64},{64,96},{96,128},{128,160},{160,192},{192,224},{1,3... | collective-permute-start | bytes 10760 | tf_op jit(solution)/shard_map/ppermute | solution.py:20
  179.1 8.9 %collective-permute-start.19 = (f32[28,1,130]{2,1,0:T(1,128)S(1)}, f32[28,1,130]{2,1,0:T(1,128)S(1)}, u32[]{:S(2)}, u32[]{:S(2)}) collective-permute-start(f32[28,1,130]{2,1,0:T(1,128)S(1)} %get-tuple-element.30), channel_id=1, source_target_pairs={{0,1},{1,2},{2,3},{3,4},{4,5},{5,6},{6,7},{7,8},{8,9},{9,10},{10,1... | collective-permute-start | bytes 43688 | tf_op jit(solution)/shard_map/ppermute | solution.py:20
  189.3 15.1 %collective-permute-start.21 = (f32[28,32,1]{2,1,0:T(8,128)S(1)}, f32[28,32,1]{2,1,0:T(8,128)S(1)}, u32[]{:S(2)}, u32[]{:S(2)}) collective-permute-start(f32[28,32,1]{2,1,0:T(8,128)S(1)} %get-tuple-element.49), channel_id=1, source_target_pairs={{32,0},{64,32},{96,64},{128,96},{160,128},{192,160},{224,192},{33,... | collective-permute-start | bytes 10760 | tf_op jit(solution)/shard_map/ppermute | solution.py:22
  191.3 14.4 %collective-permute-start.20 = (f32[28,32,1]{2,1,0:T(8,128)S(1)}, f32[28,32,1]{2,1,0:T(8,128)S(1)}, u32[]{:S(2)}, u32[]{:S(2)}) collective-permute-start(f32[28,32,1]{2,1,0:T(8,128)S(1)} %get-tuple-element.50), channel_id=1, source_target_pairs={{0,32},{32,64},{64,96},{96,128},{128,160},{160,192},{192,224},{1,3... | collective-permute-start | bytes 10760 | tf_op jit(solution)/shard_map/ppermute | solution.py:20
  208.1 8.9 %collective-permute-start.23 = (f32[28,1,130]{2,1,0:T(1,128)S(1)}, f32[28,1,130]{2,1,0:T(1,128)S(1)}, u32[]{:S(2)}, u32[]{:S(2)}) collective-permute-start(f32[28,1,130]{2,1,0:T(1,128)S(1)} %get-tuple-element.28), channel_id=1, source_target_pairs={{0,1},{1,2},{2,3},{3,4},{4,5},{5,6},{6,7},{7,8},{8,9},{9,10},{10,1... | collective-permute-start | bytes 43688 | tf_op jit(solution)/shard_map/ppermute | solution.py:20
  218.3 16.4 %collective-permute-start.25 = (f32[28,32,1]{2,1,0:T(8,128)S(1)}, f32[28,32,1]{2,1,0:T(8,128)S(1)}, u32[]{:S(2)}, u32[]{:S(2)}) collective-permute-start(f32[28,32,1]{2,1,0:T(8,128)S(1)} %get-tuple-element.45), channel_id=1, source_target_pairs={{32,0},{64,32},{96,64},{128,96},{160,128},{192,160},{224,192},{33,... | collective-permute-start | bytes 10760 | tf_op jit(solution)/shard_map/ppermute | solution.py:22
  220.2 16.0 %collective-permute-start.24 = (f32[28,32,1]{2,1,0:T(8,128)S(1)}, f32[28,32,1]{2,1,0:T(8,128)S(1)}, u32[]{:S(2)}, u32[]{:S(2)}) collective-permute-start(f32[28,32,1]{2,1,0:T(8,128)S(1)} %get-tuple-element.46), channel_id=1, source_target_pairs={{0,32},{32,64},{64,96},{96,128},{128,160},{160,192},{192,224},{1,3... | collective-permute-start | bytes 10760 | tf_op jit(solution)/shard_map/ppermute | solution.py:20
  238.4 8.9 %collective-permute-start.27 = (f32[28,1,130]{2,1,0:T(1,128)S(1)}, f32[28,1,130]{2,1,0:T(1,128)S(1)}, u32[]{:S(2)}, u32[]{:S(2)}) collective-permute-start(f32[28,1,130]{2,1,0:T(1,128)S(1)} %get-tuple-element.26), channel_id=1, source_target_pairs={{0,1},{1,2},{2,3},{3,4},{4,5},{5,6},{6,7},{7,8},{8,9},{9,10},{10,1... | collective-permute-start | bytes 43688 | tf_op jit(solution)/shard_map/ppermute | solution.py:20
  248.6 16.6 %collective-permute-start.29 = (f32[28,32,1]{2,1,0:T(8,128)S(1)}, f32[28,32,1]{2,1,0:T(8,128)S(1)}, u32[]{:S(2)}, u32[]{:S(2)}) collective-permute-start(f32[28,32,1]{2,1,0:T(8,128)S(1)} %get-tuple-element.39), channel_id=1, source_target_pairs={{32,0},{64,32},{96,64},{128,96},{160,128},{192,160},{224,192},{33,... | collective-permute-start | bytes 10760 | tf_op jit(solution)/shard_map/ppermute | solution.py:22
  250.5 17.0 %collective-permute-start.28 = (f32[28,32,1]{2,1,0:T(8,128)S(1)}, f32[28,32,1]{2,1,0:T(8,128)S(1)}, u32[]{:S(2)}, u32[]{:S(2)}) collective-permute-start(f32[28,32,1]{2,1,0:T(8,128)S(1)} %get-tuple-element.40), channel_id=1, source_target_pairs={{0,32},{32,64},{64,96},{96,128},{128,160},{160,192},{192,224},{1,3... | collective-permute-start | bytes 10760 | tf_op jit(solution)/shard_map/ppermute | solution.py:20
  (16 other events, 184.9 us)
where the time goes:
time: 285 us; the launch traced here: 280 us
  waiting for transfers between devices  141 us (49%)
  starting transfers between devices  99.4 us (35%)
  other arithmetic  32.5 us (11%)
  local copies, waits for them, and re-layouts  6.2 us (2%)
    ppermute x16, waiting for transfers between devices, padded(): lax.ppermute(tail, axis, [(i, (i + 1) % count) for i in range(ends)])  75 us
    ppermute x16, waiting for transfers between devices, padded(): lax.ppermute(head, axis, [((i + 1) % count, i) for i in range(ends)])  66.2 us
    ppermute x16, starting transfers between devices, padded(): lax.ppermute(tail, axis, [(i, (i + 1) % count) for i in range(ends)])  55.1 us
    ppermute x16, starting transfers between devices, padded(): lax.ppermute(head, axis, [((i + 1) % count, i) for i in range(ends)])  44.3 us
    div x7, other arithmetic, update(): newer = (source + beta * older - weight * state) / (1.0 + beta)  28.6 us
  transfers between devices with their start and end apart: 32, of which 24 were waited for; matrix products, arithmetic and copies ran while one was open for 1% of the time, Pallas kernels for 0%

commit v1 on v0

v1 whole, which is shorter than its diff:
```python
import jax
import jax.numpy as jnp
from jax import lax
from jax.experimental import pallas as pl
from jax.experimental.pallas import tpu as pltpu
from jax.sharding import PartitionSpec as P

ITERS = 8
NZ = 28
ROWS = 32
LANES = 128
H = 8
GROUPS = 4
PLANES = 7
BUF = ROWS + 4 * H
TALL = ROWS + 2 * H
COURANT = 0.33
K0 = (2.0 - 6.0 * COURANT) / COURANT
K1 = 2.0 / COURANT
AIR = 8
OUTSIDE = 9
OFFSET = (0, 8, 64, 72)
MESH = pl.DeviceIdType.MESH
F32 = jnp.float32


def roll(value, shift):
    shift %= LANES
    return value if shift == 0 else pltpu.roll(value, shift, axis=1)


def lane_ids():
    return lax.broadcasted_iota(jnp.int32, (8, LANES), 1)


def class_tables(table):
    lane = lane_ids()
    rows = []
    for row, air in ((0, 0.0), (1, 0.0), (2, 1.0), (3, 0.0)):
        picked = jnp.full((8, LANES), air, F32)
        for index in range(8):
            picked = jnp.where(lane == index, table[row, index], picked)
        rows.append(picked)
    loss = 1.0 / (1.0 + rows[0])
    source = jnp.where(lane == OUTSIDE, 0.0, COURANT * loss)
    return (source, rows[1] * loss, rows[2], rows[3])


def look_up(tables, cells):
    index = cells.astype(jnp.int32)
    return [jnp.take_along_axis(t, index, axis=1, mode="promise_in_bounds") for t in tables]


def cell_step(centre, around, older, state, source, weight, decay, couple):
    moved = source * (around + K0 * centre - K1 * older) - weight * state
    return older + moved, decay * state + couple * moved


def kernel(
    n_x, n_y,
    p_in, q_in, v_in, mask_in, mat_in, low_in, high_in, table,
    p_out, v_out,
    field_a, field_b, field_c, state_a, state_b, cls, coef, mask, mat,
    m_left, m_right, r_left, r_right,
    s_field_a, s_field_b, s_field_c, s_state_a, s_state_b, s_coef, s_ghost, edge,
    load_sem, send_sem, recv_sem,
):
    field, state = (field_a, field_b, field_c), (state_a, state_b)
    s_field, s_state = (s_field_a, s_field_b, s_field_c), (s_state_a, s_state_b)
    gx, gy = lax.axis_index("gx"), lax.axis_index("gy")

    def there(dx, dy):
        x, y = gx + dx, gy + dy
        return (x >= 0) & (x < n_x) & (y >= 0) & (y < n_y)

    around = [(dx, dy) for dx in (-1, 0, 1) for dy in (-1, 0, 1) if dx or dy]
    barrier = pltpu.get_barrier_semaphore()
    count = jnp.int32(0)
    for dx, dy in around:
        ok = there(dx, dy)
        count = count + ok.astype(jnp.int32)

        @pl.when(ok)
        def _():
            pl.semaphore_signal(barrier, inc=1, device_id=(gx + dx, gy + dy), device_id_type=MESH)

    own = pl.ds(2 * H, ROWS)
    loads = [
        pltpu.make_async_copy(src, dst, load_sem.at[i])
        for i, (src, dst) in enumerate(
            [
                (p_in, field[0].at[pl.ds(1, NZ), own]),
                (q_in, field[1].at[pl.ds(1, NZ), own]),
                (v_in, state[0].at[:, own]),
                (mask_in, mask),
                (mat_in, mat),
                (low_in, field[0].at[0, own]),
                (high_in, field[0].at[NZ + 1, own]),
            ]
        )
    ]
    for load in loads:
        load.start()

    lane = lane_ids()
    place = lane % 16
    tables = class_tables(table)
    for load in loads:
        load.wait()

    @pl.loop(0, NZ)
    def _(z):
        for k in range(4):
            rows = pl.ds(8 * k, 8)
            wall = mask[z, rows, :] == 1
            cls[z, pl.ds(16 + 8 * k, 8), :] = jnp.where(wall, mat[z, rows, :], AIR).astype(F32)

    def pack(out, first, spare, ghost_shift):
        @pl.loop(0, PLANES)
        def _(j):
            for k in range(4):
                rows = pl.ds(16 + 8 * k, 8)
                total = jnp.zeros((8, LANES), F32)
                for a in range(4):
                    for g in range(GROUPS):
                        z = 7 * g + j
                        if a == 0:
                            value = field[0][z + 1, rows, :]
                        elif a == 1:
                            value = field[1][z + 1, rows, :]
                        elif a == 2:
                            value = state[0][z, rows, :]
                        else:
                            value = cls[z, rows, :]
                        to = OFFSET[a] + 16 * g
                        total = jnp.where((lane >= to) & (lane < to + 8), roll(value, to - first), total)
                out[j, pl.ds(8 + 8 * k, 8), :] = total

        for j in range(PLANES):
            at = first + j + ghost_shift
            for k in range(4):
                rows, into = pl.ds(16 + 8 * k, 8), pl.ds(8 + 8 * k, 8)
                low_at, high_at = OFFSET[1] + spare, OFFSET[1] + 48 + spare
                value = out[j, into, :]
                value = jnp.where(lane == low_at, roll(field[0][0, rows, :], low_at - at), value)
                value = jnp.where(lane == high_at, roll(field[0][NZ + 1, rows, :], high_at - at), value)
                out[j, into, :] = value

    pack(m_left, 0, 7, 0)
    pack(m_right, LANES - 8, 0, 1)

    pl.semaphore_wait(barrier, count)

    transfers = []

    def transfer(src, dst, dx, dy):
        i = len(transfers)
        copy = pltpu.make_async_remote_copy(
            src_ref=src, dst_ref=dst, send_sem=send_sem.at[i], recv_sem=recv_sem.at[i],
            device_id=(gx + dx, gy + dy), device_id_type=MESH,
        )
        transfers.append((copy, dx, dy))

    for dx, message, into in ((1, m_right, r_left), (-1, m_left, r_right)):
        transfer(message.at[:, pl.ds(8, ROWS)], into.at[:, pl.ds(8, ROWS)], dx, 0)
    for dy, main_from, main_to, part_from, part_to in ((1, 40, 8, 32, 0), (-1, 16, 48, 8, 40)):
        for dx, message, into in ((1, m_right, r_left), (-1, m_left, r_right)):
            transfer(message.at[:, pl.ds(part_from, 8)], into.at[:, pl.ds(part_to, 8)], dx, dy)
        src, dst = pl.ds(main_from, 8), pl.ds(main_to, 8)
        transfer(field[0].at[:, src], field[0].at[:, dst], 0, dy)
        transfer(field[1].at[pl.ds(1, NZ), src], field[1].at[pl.ds(1, NZ), dst], 0, dy)
        transfer(state[0].at[:, src], state[0].at[:, dst], 0, dy)
        transfer(cls.at[:, src], cls.at[:, dst], 0, dy)
        for message in (m_left, m_right):
            transfer(message.at[:, pl.ds(part_from, 8)], message.at[:, pl.ds(part_to, 8)], 0, dy)

    for copy, dx, dy in transfers:

        @pl.when(there(dx, dy))
        def _():
            copy.start()

    nothing = jnp.where((lane >= 64) & (place >= 8), float(OUTSIDE), 0.0).astype(F32)

    def blank(ref, first, rows):
        @pl.loop(0, PLANES)
        def _(j):
            for k in range(rows // 8):
                ref[j, pl.ds(first + 8 * k, 8), :] = nothing

    for dy, main, part in ((-1, 8, 0), (1, 48, 40)):

        @pl.when(jnp.logical_not(there(0, dy)))
        def _():
            rows = pl.ds(main, 8)
            zero = jnp.zeros((8, LANES), F32)
            field[0][0, rows, :] = zero
            field[0][NZ + 1, rows, :] = zero

            @pl.loop(0, NZ)
            def _(z):
                field[0][z + 1, rows, :] = zero
                field[1][z + 1, rows, :] = zero
                state[0][z, rows, :] = zero
                cls[z, rows, :] = jnp.full((8, LANES), float(OUTSIDE), F32)

            blank(m_left, part, 8)
            blank(m_right, part, 8)

        for dx, ref in ((-1, r_left), (1, r_right)):

            @pl.when(there(dx, 0) & jnp.logical_not(there(0, dy)))
            def _():
                blank(ref, part, 8)

    for dx, ref in ((-1, r_left), (1, r_right)):

        @pl.when(jnp.logical_not(there(dx, 0)))
        def _():
            blank(ref, 0, TALL)

    def coefficients(k):
        @pl.loop(0, NZ)
        def _(z):
            rows = pl.ds(8 + 8 * k, 8)
            for i, value in enumerate(look_up(tables, cls[z, rows, :])):
                coef[i, z, rows, :] = value

    for k in (1, 2, 3, 4):
        coefficients(k)

    for copy, dx, dy in transfers:

        @pl.when(there(-dx, -dy))
        def _():
            copy.wait_recv()

    for copy, dx, dy in transfers:

        @pl.when(there(dx, dy))
        def _():
            copy.wait_send()

    coefficients(0)
    coefficients(5)
    for k in range(6):
        rows = pl.ds(8 + 8 * k, 8)
        for plane in (0, NZ + 1):
            ghost = field[0][plane, rows, :]
            field[1][plane, rows, :] = ghost
            field[2][plane, rows, :] = ghost

    side, half = lane >= 64, place >= 8

    def gather_strip(a, j, rows):
        at = OFFSET[a]
        lower = jnp.where(half, roll(m_left[j, rows, :], 8 - at), roll(r_left[j, rows, :], -at))
        upper = jnp.where(half, roll(r_right[j, rows, :], 72 - at), roll(m_right[j, rows, :], 64 - at))
        return jnp.where(side, upper, lower)

    @pl.loop(0, PLANES)
    def _(j):
        for k in range(6):
            rows, into = pl.ds(8 * k, 8), pl.ds(8 + 8 * k, 8)
            s_field[0][j + 1, into, :] = gather_strip(0, j, rows)
            s_field[1][j + 1, into, :] = gather_strip(1, j, rows)
            s_state[0][j, into, :] = gather_strip(2, j, rows)
            for i, value in enumerate(look_up(tables, gather_strip(3, j, rows))):
                s_coef[i, j, into, :] = value

    for k in range(6):
        rows = pl.ds(8 * k, 8)
        total = jnp.zeros((8, LANES), F32)
        for j in range(PLANES):
            for ref, spare, to in ((r_left, 0, 1), (m_left, 7, 8), (m_right, 0, 65), (r_right, 7, 72)):
                value = roll(ref[j, rows, :], to + j - OFFSET[1] - spare)
                total = jnp.where((lane == to + j) | (lane == to + j + 48), value, total)
        s_ghost[pl.ds(8 + 8 * k, 8), :] = total

    group = (lane // 16) % 4

    def strip_ends(now):
        for k in range(6):
            rows = pl.ds(8 + 8 * k, 8)
            ghost = s_ghost[rows, :]
            s_field[now][0, rows, :] = jnp.where(group == 0, ghost, roll(s_field[now][PLANES, rows, :], 16))
            s_field[now][PLANES + 1, rows, :] = jnp.where(group == 3, ghost, roll(s_field[now][1, rows, :], -16))

    strip_ends(0)
    mark = place == 6

    def column(ref, plane, blocks):
        return [
            (ref[plane, pl.ds(8 + 8 * k, 8), :], ref[plane, pl.ds(7 + 8 * k, 8), :] + ref[plane, pl.ds(9 + 8 * k, 8), :])
            for k in blocks
        ]

    def strip_step(p, q, out, v, v_out, blocks):
        @pl.loop(0, PLANES, unroll=7)
        def _(j):
            done = []
            for k, (centre, y_sum) in zip(blocks, column(p, j + 1, blocks)):
                rows = pl.ds(8 + 8 * k, 8)
                edge[j, rows, :] = jnp.where(mark, roll(centre, -66), centre)
                total = (roll(centre, 1) + roll(centre, -1)) + y_sum + (p[j, rows, :] + p[j + 2, rows, :])
                done.append((rows,) + cell_step(
                    centre, total, q[j + 1, rows, :], v[j, rows, :], *[s_coef[i, j, rows, :] for i in range(4)],
                ))
            for rows, newer, filt in done:
                out[j + 1, rows, :] = newer
                v_out[j, rows, :] = filt

    first_lane, last_lane = lane == 0, lane == LANES - 1

    def main_step(p, q, v, blocks, store):
        for g in range(GROUPS):

            @pl.loop(0, PLANES, unroll=7)
            def _(j):
                z = 7 * g + j
                done = []
                for k, (centre, y_sum) in zip(blocks, column(p, z + 1, blocks)):
                    rows = pl.ds(8 + 8 * k, 8)
                    beside = roll(edge[j, rows, :], -(16 * g + 7))
                    total = (
                        (jnp.where(first_lane, beside, roll(centre, 1)) + jnp.where(last_lane, beside, roll(centre, -1)))
                        + y_sum
                        + (p[z, rows, :] + p[z + 2, rows, :])
                    )
                    done.append((k,) + cell_step(
                        centre, total, q[z + 1, rows, :], v[z, rows, :], *[coef[i, z, rows, :] for i in range(4)],
                    ))
                for k, newer, filt in done:
                    store(z, k, newer, filt)

    every, inner = range(6), range(1, 5)
    for step in range(ITERS):
        now, old, new = [(0, 1, 2), (2, 0, 1), (1, 2, 0)][step % 3]
        v, v_new = state[step % 2], state[1 - step % 2]
        last = step == ITERS - 1
        strip_step(s_field[now], s_field[old], s_field[new], s_state[step % 2], s_state[1 - step % 2], inner if last else every)
        if not last:
            strip_ends(new)

        def store(z, k, newer, filt):
            rows = pl.ds(8 + 8 * k, 8)
            field[new][z + 1, rows, :] = newer
            v_new[z, rows, :] = filt

        def store_out(z, k, newer, filt):
            rows = pl.ds(8 * k - 8, 8)
            p_out[z, rows, :] = newer
            v_out[z, rows, :] = filt

        main_step(field[now], field[old], v, inner if last else every, store_out if last else store)


def solution(mesh):
    n_x, n_y = mesh.shape["gx"], mesh.shape["gy"]

    def body(*args):
        hbm = pl.BlockSpec(memory_space=pltpu.HBM)
        vmem = pl.BlockSpec(memory_space=pltpu.VMEM)
        big = (NZ, BUF, LANES)
        strip = (PLANES, BUF, LANES)
        message = pltpu.VMEM((PLANES, TALL, LANES), F32)
        tall, s_tall = (pltpu.VMEM((n + 2, BUF, LANES), F32) for n in (NZ, PLANES))
        n_transfers = 18
        return pl.pallas_call(
            lambda *refs: kernel(n_x, n_y, *refs),
            out_shape=[pltpu.VMEM((NZ, ROWS, LANES), F32)] * 2,
            in_specs=[hbm] * 7 + [pl.BlockSpec(memory_space=pltpu.SMEM)],
            out_specs=[vmem] * 2,
            scratch_shapes=[
                tall, tall, tall,
                pltpu.VMEM(big, F32),
                pltpu.VMEM(big, F32),
                pltpu.VMEM(big, F32),
                pltpu.VMEM((4,) + big, F32),
                pltpu.VMEM((NZ, ROWS, LANES), jnp.int32),
                pltpu.VMEM((NZ, ROWS, LANES), jnp.int32),
                message, message, message, message,
                s_tall, s_tall, s_tall,
                pltpu.VMEM(strip, F32),
                pltpu.VMEM(strip, F32),
                pltpu.VMEM((4,) + strip, F32),
                pltpu.VMEM((BUF, LANES), F32),
                pltpu.VMEM(strip, F32),
                pltpu.SemaphoreType.DMA((7,)),
                pltpu.SemaphoreType.DMA((n_transfers,)),
                pltpu.SemaphoreType.DMA((n_transfers,)),
            ],
            compiler_params=pltpu.CompilerParams(
                collective_id=1, has_side_effects=True, vmem_limit_bytes=62 * 1024 * 1024
            ),
        )(*args)

    spec = P(None, "gy", "gx")
    return jax.shard_map(
        body,
        mesh=mesh,
        in_specs=(spec,) * 5 + (P("gy", "gx"),) * 2 + (P(),),
        out_specs=(spec, spec),
        check_vma=False,
    )
```

time: 285 us -> 35 us (0.12)
  the two profiles are of different devices: /device:TPU:22 before, /device:TPU:1 now
where the time goes in v1:
time: 35 us; the launch traced here: 34.9 us
  Pallas kernels  32.7 us (93%)
  local copies, waits for them, and re-layouts  1.54 us (4%)
  between operations  0.64 us (2%)
    pallas_call x1, Pallas kernels, body(): pl.pallas_call(lambda *refs: kernel(n_x, n_y, *refs), out_shape=[pltpu.VM...  32.7 us
    unnamed x2, local copies, waits for them, and re-layouts  1.54 us

profile of v1, /device:TPU:1, one launch (start us, length us, event | category | flops | bytes accessed | tf_op | source)
XLA Modules:
  0.0 34.9 jit_solution(9716266274843036491)
XLA Ops:
  0.6 32.7 %shard_map.95 = (f32[28,32,128]{2,1,0:T(8,128)S(1)}, f32[28,32,128]{2,1,0:T(8,128)S(1)}) custom-call(f32[28,32,128]{2,1,0:T(8,128)} %refs_0_.1, f32[28,32,128]{2,1,0:T(8,128)} %refs_1_.1, f32[28,32,128]{2,1,0:T(8,128)} %refs_2_.1, s32[28,32,128]{2,1,0:T(8,128)} %refs_3_.1, s32[28,32,128]{2,1,0:T(8,128)} %refs_4_.1, f32[32,128]{1,0:T(8,128)} %refs_5_.1, ...), custom_call_target="tpu_custom_call" | custom-call | tf_op jit(solution)/shard_map/pallas_call | solution.py:369
  33.3 0.8 %copy.12 = f32[28,32,128]{2,1,0:T(8,128)} copy(f32[28,32,128]{2,1,0:T(8,128)S(1)} %get-tuple-element.2) | data formatting | bytes 917504
  34.1 0.8 %copy.13 = f32[28,32,128]{2,1,0:T(8,128)} copy(f32[28,32,128]{2,1,0:T(8,128)S(1)} %get-tuple-element.3) | data formatting | bytes 917504

commit v2 on v1

--- a/solution.py
+++ b/solution.py
@@ -60,13 +60,13 @@
     n_x, n_y,
     p_in, q_in, v_in, mask_in, mat_in, low_in, high_in, table,
     p_out, v_out,
-    field_a, field_b, field_c, state_a, state_b, cls, coef, mask, mat,
+    field_a, field_b, state_a, cls, coef, mask, mat,
     m_left, m_right, r_left, r_right,
-    s_field_a, s_field_b, s_field_c, s_state_a, s_state_b, s_coef, s_ghost, edge,
+    s_field_a, s_field_b, s_state_a, s_coef, s_ghost, edge,
     load_sem, send_sem, recv_sem,
 ):
-    field, state = (field_a, field_b, field_c), (state_a, state_b)
-    s_field, s_state = (s_field_a, s_field_b, s_field_c), (s_state_a, s_state_b)
+    field, state = (field_a, field_b), (state_a,)
+    s_field, s_state = (s_field_a, s_field_b), (s_state_a,)
     gx, gy = lax.axis_index("gx"), lax.axis_index("gy")
 
     def there(dx, dy):
@@ -108,43 +108,37 @@
     for load in loads:
         load.wait()
 
-    @pl.loop(0, NZ)
+    @pl.loop(0, NZ, unroll=7)
     def _(z):
         for k in range(4):
             rows = pl.ds(8 * k, 8)
             wall = mask[z, rows, :] == 1
             cls[z, pl.ds(16 + 8 * k, 8), :] = jnp.where(wall, mat[z, rows, :], AIR).astype(F32)
 
+    def merge(bit, low, high):
+        return jnp.where((lane & bit) != 0, high, low)
+
     def pack(out, first, spare, ghost_shift):
-        @pl.loop(0, PLANES)
-        def _(j):
+        def column(a, z, rows):
+            ref, plane = ((field[0], z + 1), (field[1], z + 1), (state[0], z), (cls, z))[a]
+            return ref[plane, rows, :]
+
+        for j in range(PLANES):
+            at = first + j + ghost_shift
+            low_at, high_at = OFFSET[1] + spare, OFFSET[1] + 48 + spare
             for k in range(4):
                 rows = pl.ds(16 + 8 * k, 8)
-                total = jnp.zeros((8, LANES), F32)
-                for a in range(4):
-                    for g in range(GROUPS):
-                        z = 7 * g + j
-                        if a == 0:
-                            value = field[0][z + 1, rows, :]
-                        elif a == 1:
-                            value = field[1][z + 1, rows, :]
-                        elif a == 2:
-                            value = state[0][z, rows, :]
-                        else:
-                            value = cls[z, rows, :]
-                        to = OFFSET[a] + 16 * g
-                        total = jnp.where((lane >= to) & (lane < to + 8), roll(value, to - first), total)
-                out[j, pl.ds(8 + 8 * k, 8), :] = total
-
-        for j in range(PLANES):
-            at = first + j + ghost_shift
-            for k in range(4):
-                rows, into = pl.ds(16 + 8 * k, 8), pl.ds(8 + 8 * k, 8)
-                low_at, high_at = OFFSET[1] + spare, OFFSET[1] + 48 + spare
-                value = out[j, into, :]
-                value = jnp.where(lane == low_at, roll(field[0][0, rows, :], low_at - at), value)
-                value = jnp.where(lane == high_at, roll(field[0][NZ + 1, rows, :], high_at - at), value)
-                out[j, into, :] = value
+                parts = [
+                    [roll(column(a, 7 * g + j, rows), OFFSET[a] + 16 * g - first) for g in range(GROUPS)]
+                    for a in range(4)
+                ]
+                parts[1][0] = jnp.where(lane == low_at, roll(field[0][0, rows, :], low_at - at), parts[1][0])
+                parts[1][3] = jnp.where(lane == high_at, roll(field[0][NZ + 1, rows, :], high_at - at), parts[1][3])
+                halves = []
+                for a in (0, 2):
+                    g = [merge(8, parts[a][g], parts[a + 1][g]) for g in range(GROUPS)]
+                    halves.append(merge(32, merge(16, g[0], g[1]), merge(16, g[2], g[3])))
+                out[j, pl.ds(8 + 8 * k, 8), :] = merge(64, halves[0], halves[1])
 
     pack(m_left, 0, 7, 0)
     pack(m_right, LANES - 8, 0, 1)
@@ -153,13 +147,13 @@
 
     transfers = []
 
-    def transfer(src, dst, dx, dy):
+    def transfer(src, dst, dx, dy, heavy=False):
         i = len(transfers)
         copy = pltpu.make_async_remote_copy(
             src_ref=src, dst_ref=dst, send_sem=send_sem.at[i], recv_sem=recv_sem.at[i],
             device_id=(gx + dx, gy + dy), device_id_type=MESH,
         )
-        transfers.append((copy, dx, dy))
+        transfers.append((copy, dx, dy, heavy))
 
     for dx, message, into in ((1, m_right, r_left), (-1, m_left, r_right)):
         transfer(message.at[:, pl.ds(8, ROWS)], into.at[:, pl.ds(8, ROWS)], dx, 0)
@@ -172,11 +166,17 @@
         transfer(state[0].at[:, src], state[0].at[:, dst], 0, dy)
         transfer(cls.at[:, src], cls.at[:, dst], 0, dy)
         for message in (m_left, m_right):
-            transfer(message.at[:, pl.ds(part_from, 8)], message.at[:, pl.ds(part_to, 8)], 0, dy)
-
-    for copy, dx, dy in transfers:
-
-        @pl.when(there(dx, dy))
+            transfer(message.at[:, pl.ds(part_from, 8)], message.at[:, pl.ds(part_to, 8)], 0, dy, dy > 0)
+
+    def long_step(dy):
+        return gy + max(dy, 0) == n_y // 2
+
+    for copy, dx, dy, heavy in transfers:
+        at_once = there(dx, dy)
+        if heavy:
+            at_once = at_once & jnp.logical_not(long_step(dy))
+
+        @pl.when(at_once)
         def _():
             copy.start()
 
@@ -219,46 +219,47 @@
         def _():
             blank(ref, 0, TALL)
 
-    def coefficients(k):
-        @pl.loop(0, NZ)
+    def coefficients(blocks):
+        @pl.loop(0, NZ, unroll=7)
         def _(z):
-            rows = pl.ds(8 + 8 * k, 8)
-            for i, value in enumerate(look_up(tables, cls[z, rows, :])):
-                coef[i, z, rows, :] = value
-
-    for k in (1, 2, 3, 4):
-        coefficients(k)
-
-    for copy, dx, dy in transfers:
-
-        @pl.when(there(-dx, -dy))
-        def _():
-            copy.wait_recv()
-
-    for copy, dx, dy in transfers:
-
-        @pl.when(there(dx, dy))
-        def _():
-            copy.wait_send()
-
-    coefficients(0)
-    coefficients(5)
+            for k in blocks:
+                rows = pl.ds(8 + 8 * k, 8)
+                for i, value in enumerate(look_up(tables, cls[z, rows, :])):
+                    coef[i, z, rows, :] = value
+
+    coefficients((1, 2, 3, 4))
+
+    def receive(of_x):
+        for copy, dx, dy, _ in transfers:
+            if (dy == 0) == of_x:
+
+                @pl.when(there(-dx, -dy))
+                def _():
+                    copy.wait_recv()
+
+    receive(True)
+    for copy, dx, dy, heavy in transfers:
+        if heavy:
+
+            @pl.when(there(dx, dy) & long_step(dy))
+            def _():
+                copy.start()
+
+    receive(False)
+    coefficients((0, 5))
     for k in range(6):
         rows = pl.ds(8 + 8 * k, 8)
         for plane in (0, NZ + 1):
             ghost = field[0][plane, rows, :]
             field[1][plane, rows, :] = ghost
-            field[2][plane, rows, :] = ghost
-
-    side, half = lane >= 64, place >= 8
 
     def gather_strip(a, j, rows):
         at = OFFSET[a]
-        lower = jnp.where(half, roll(m_left[j, rows, :], 8 - at), roll(r_left[j, rows, :], -at))
-        upper = jnp.where(half, roll(r_right[j, rows, :], 72 - at), roll(m_right[j, rows, :], 64 - at))
-        return jnp.where(side, upper, lower)
-
-    @pl.loop(0, PLANES)
+        lower = merge(8, roll(r_left[j, rows, :], -at), roll(m_left[j, rows, :], 8 - at))
+        upper = merge(8, roll(m_right[j, rows, :], 64 - at), roll(r_right[j, rows, :], 72 - at))
+        return merge(64, lower, upper)
+
+    @pl.loop(0, PLANES, unroll=7)
     def _(j):
         for k in range(6):
             rows, into = pl.ds(8 * k, 8), pl.ds(8 + 8 * k, 8)
@@ -279,80 +280,94 @@
 
     group = (lane // 16) % 4
 
-    def strip_ends(now):
+    def strip_ends(ref):
         for k in range(6):
             rows = pl.ds(8 + 8 * k, 8)
             ghost = s_ghost[rows, :]
-            s_field[now][0, rows, :] = jnp.where(group == 0, ghost, roll(s_field[now][PLANES, rows, :], 16))
-            s_field[now][PLANES + 1, rows, :] = jnp.where(group == 3, ghost, roll(s_field[now][1, rows, :], -16))
-
-    strip_ends(0)
+            ref[0, rows, :] = jnp.where(group == 0, ghost, roll(ref[PLANES, rows, :], 16))
+            ref[PLANES + 1, rows, :] = jnp.where(group == 3, ghost, roll(ref[1, rows, :], -16))
+
+    strip_ends(s_field[0])
     mark = place == 6
 
-    def column(ref, plane, blocks):
-        return [
-            (ref[plane, pl.ds(8 + 8 * k, 8), :], ref[plane, pl.ds(7 + 8 * k, 8), :] + ref[plane, pl.ds(9 + 8 * k, 8), :])
-            for k in blocks
-        ]
-
-    def strip_step(p, q, out, v, v_out, blocks):
-        @pl.loop(0, PLANES, unroll=7)
-        def _(j):
+
+    def y_sum(ref, plane, k):
+        return ref[plane, pl.ds(7 + 8 * k, 8), :] + ref[plane, pl.ds(9 + 8 * k, 8), :]
+
+    def strip_step(p, q, blocks):
+        for j in range(PLANES):
             done = []
-            for k, (centre, y_sum) in zip(blocks, column(p, j + 1, blocks)):
+            for k in blocks:
                 rows = pl.ds(8 + 8 * k, 8)
+                centre = p[j + 1, rows, :]
                 edge[j, rows, :] = jnp.where(mark, roll(centre, -66), centre)
-                total = (roll(centre, 1) + roll(centre, -1)) + y_sum + (p[j, rows, :] + p[j + 2, rows, :])
+                total = (roll(centre, 1) + roll(centre, -1)) + y_sum(p, j + 1, k) + (p[j, rows, :] + p[j + 2, rows, :])
                 done.append((rows,) + cell_step(
-                    centre, total, q[j + 1, rows, :], v[j, rows, :], *[s_coef[i, j, rows, :] for i in range(4)],
+                    centre, total, q[j + 1, rows, :], s_state[0][j, rows, :], *[s_coef[i, j, rows, :] for i in range(4)],
                 ))
             for rows, newer, filt in done:
-                out[j + 1, rows, :] = newer
-                v_out[j, rows, :] = filt
+                q[j + 1, rows, :] = newer
+                s_state[0][j, rows, :] = filt
 
     first_lane, last_lane = lane == 0, lane == LANES - 1
 
-    def main_step(p, q, v, blocks, store):
-        for g in range(GROUPS):
-
-            @pl.loop(0, PLANES, unroll=7)
-            def _(j):
+    def main_step(p, q, blocks, store):
+        def group_step(g):
+            shift = LANES - 7 - 16 * g
+            for j in range(PLANES):
                 z = 7 * g + j
                 done = []
-                for k, (centre, y_sum) in zip(blocks, column(p, z + 1, blocks)):
+                for k in blocks:
                     rows = pl.ds(8 + 8 * k, 8)
-                    beside = roll(edge[j, rows, :], -(16 * g + 7))
+                    centre = p[z + 1, rows, :]
+                    beside = pltpu.roll(edge[j, rows, :], shift, axis=1)
                     total = (
                         (jnp.where(first_lane, beside, roll(centre, 1)) + jnp.where(last_lane, beside, roll(centre, -1)))
-                        + y_sum
+                        + y_sum(p, z + 1, k)
                         + (p[z, rows, :] + p[z + 2, rows, :])
                     )
                     done.append((k,) + cell_step(
-                        centre, total, q[z + 1, rows, :], v[z, rows, :], *[coef[i, z, rows, :] for i in range(4)],
+                        centre, total, q[z + 1, rows, :], state[0][z, rows, :], *[coef[i, z, rows, :] for i in range(4)],
                     ))
                 for k, newer, filt in done:
                     store(z, k, newer, filt)
 
+        for g in range(GROUPS):
+            group_step(g)
+
     every, inner = range(6), range(1, 5)
-    for step in range(ITERS):
-        now, old, new = [(0, 1, 2), (2, 0, 1), (1, 2, 0)][step % 3]
-        v, v_new = state[step % 2], state[1 - step % 2]
-        last = step == ITERS - 1
-        strip_step(s_field[now], s_field[old], s_field[new], s_state[step % 2], s_state[1 - step % 2], inner if last else every)
-        if not last:
-            strip_ends(new)
+
+    def step(p, q, sp, sq):
+        strip_step(sp, sq, every)
+        strip_ends(sq)
 
         def store(z, k, newer, filt):
             rows = pl.ds(8 + 8 * k, 8)
-            field[new][z + 1, rows, :] = newer
-            v_new[z, rows, :] = filt
-
-        def store_out(z, k, newer, filt):
-            rows = pl.ds(8 * k - 8, 8)
-            p_out[z, rows, :] = newer
-            v_out[z, rows, :] = filt
-
-        main_step(field[now], field[old], v, inner if last else every, store_out if last else store)
+            q[z + 1, rows, :] = newer
+            state[0][z, rows, :] = filt
+
+        main_step(p, q, every, store)
+
+    for copy, dx, dy, _ in transfers:
+
+        @pl.when(there(dx, dy))
+        def _():
+            copy.wait_send()
+
+    @pl.loop(0, ITERS // 2 - 1)
+    def _(pair):
+        step(field[0], field[1], s_field[0], s_field[1])
+        step(field[1], field[0], s_field[1], s_field[0])
+
+    step(field[0], field[1], s_field[0], s_field[1])
+    strip_step(s_field[1], s_field[0], inner)
+
+    def store_out(z, k, newer, filt):
+        rows = pl.ds(8 * k - 8, 8)
+        p_out[z, rows, :] = newer
+        v_out[z, rows, :] = filt
+
+    main_step(field[1], field[0], inner, store_out)
 
 
 def solution(mesh):
@@ -372,16 +387,14 @@
             in_specs=[hbm] * 7 + [pl.BlockSpec(memory_space=pltpu.SMEM)],
             out_specs=[vmem] * 2,
             scratch_shapes=[
-                tall, tall, tall,
-                pltpu.VMEM(big, F32),
+                tall, tall,
                 pltpu.VMEM(big, F32),
                 pltpu.VMEM(big, F32),
                 pltpu.VMEM((4,) + big, F32),
                 pltpu.VMEM((NZ, ROWS, LANES), jnp.int32),
                 pltpu.VMEM((NZ, ROWS, LANES), jnp.int32),
                 message, message, message, message,
-                s_tall, s_tall, s_tall,
-                pltpu.VMEM(strip, F32),
+                s_tall, s_tall,
                 pltpu.VMEM(strip, F32),
                 pltpu.VMEM((4,) + strip, F32),
                 pltpu.VMEM((BUF, LANES), F32),

time: 35 us -> 32.3 us (0.923)
  the two profiles are of different devices: /device:TPU:1 before, /device:TPU:22 now
where the time goes in v2:
time: 32.3 us; the launch traced here: 31.8 us
  Pallas kernels  29.7 us (92%)
  local copies, waits for them, and re-layouts  1.54 us (5%)
  between operations  0.64 us (2%)
    pallas_call x1, Pallas kernels, body(): pl.pallas_call(lambda *refs: kernel(n_x, n_y, *refs), out_shape=[pltpu.VM...  29.7 us
    unnamed x2, local copies, waits for them, and re-layouts  1.54 us

profile of v2, /device:TPU:22, one launch (start us, length us, event | category | flops | bytes accessed | tf_op | source)
XLA Modules:
  0.0 31.8 jit_solution(16430851759413517915)
XLA Ops:
  0.6 29.7 %shard_map.95 = (f32[28,32,128]{2,1,0:T(8,128)S(1)}, f32[28,32,128]{2,1,0:T(8,128)S(1)}) custom-call(f32[28,32,128]{2,1,0:T(8,128)} %refs_0_.1, f32[28,32,128]{2,1,0:T(8,128)} %refs_1_.1, f32[28,32,128]{2,1,0:T(8,128)} %refs_2_.1, s32[28,32,128]{2,1,0:T(8,128)} %refs_3_.1, s32[28,32,128]{2,1,0:T(8,128)} %refs_4_.1, f32[32,128]{1,0:T(8,128)} %refs_5_.1, ...), custom_call_target="tpu_custom_call" | custom-call | tf_op jit(solution)/shard_map/pallas_call | solution.py:384
  30.3 0.8 %copy.12 = f32[28,32,128]{2,1,0:T(8,128)} copy(f32[28,32,128]{2,1,0:T(8,128)S(1)} %get-tuple-element.2) | data formatting | bytes 917504
  31.1 0.8 %copy.13 = f32[28,32,128]{2,1,0:T(8,128)} copy(f32[28,32,128]{2,1,0:T(8,128)S(1)} %get-tuple-element.3) | data formatting | bytes 917504

commit v3 on v2

--- a/solution.py
+++ b/solution.py
@@ -147,13 +147,13 @@
 
     transfers = []
 
-    def transfer(src, dst, dx, dy, heavy=False):
+    def transfer(src, dst, dx, dy):
         i = len(transfers)
         copy = pltpu.make_async_remote_copy(
             src_ref=src, dst_ref=dst, send_sem=send_sem.at[i], recv_sem=recv_sem.at[i],
             device_id=(gx + dx, gy + dy), device_id_type=MESH,
         )
-        transfers.append((copy, dx, dy, heavy))
+        transfers.append((copy, dx, dy))
 
     for dx, message, into in ((1, m_right, r_left), (-1, m_left, r_right)):
         transfer(message.at[:, pl.ds(8, ROWS)], into.at[:, pl.ds(8, ROWS)], dx, 0)
@@ -166,17 +166,11 @@
         transfer(state[0].at[:, src], state[0].at[:, dst], 0, dy)
         transfer(cls.at[:, src], cls.at[:, dst], 0, dy)
         for message in (m_left, m_right):
-            transfer(message.at[:, pl.ds(part_from, 8)], message.at[:, pl.ds(part_to, 8)], 0, dy, dy > 0)
-
-    def long_step(dy):
-        return gy + max(dy, 0) == n_y // 2
-
-    for copy, dx, dy, heavy in transfers:
-        at_once = there(dx, dy)
-        if heavy:
-            at_once = at_once & jnp.logical_not(long_step(dy))
-
-        @pl.when(at_once)
+            transfer(message.at[:, pl.ds(part_from, 8)], message.at[:, pl.ds(part_to, 8)], 0, dy)
+
+    for copy, dx, dy in transfers:
+
+        @pl.when(there(dx, dy))
         def _():
             copy.start()
 
@@ -229,29 +223,13 @@
 
     coefficients((1, 2, 3, 4))
 
-    def receive(of_x):
-        for copy, dx, dy, _ in transfers:
-            if (dy == 0) == of_x:
+    def receive(part):
+        for copy, dx, dy in transfers:
+            if (0 if dx == 0 else 1 if dy == 0 else 2) == part:
 
                 @pl.when(there(-dx, -dy))
                 def _():
                     copy.wait_recv()
-
-    receive(True)
-    for copy, dx, dy, heavy in transfers:
-        if heavy:
-
-            @pl.when(there(dx, dy) & long_step(dy))
-            def _():
-                copy.start()
-
-    receive(False)
-    coefficients((0, 5))
-    for k in range(6):
-        rows = pl.ds(8 + 8 * k, 8)
-        for plane in (0, NZ + 1):
-            ghost = field[0][plane, rows, :]
-            field[1][plane, rows, :] = ghost
 
     def gather_strip(a, j, rows):
         at = OFFSET[a]
@@ -259,24 +237,36 @@
         upper = merge(8, roll(m_right[j, rows, :], 64 - at), roll(r_right[j, rows, :], 72 - at))
         return merge(64, lower, upper)
 
-    @pl.loop(0, PLANES, unroll=7)
-    def _(j):
-        for k in range(6):
-            rows, into = pl.ds(8 * k, 8), pl.ds(8 + 8 * k, 8)
-            s_field[0][j + 1, into, :] = gather_strip(0, j, rows)
-            s_field[1][j + 1, into, :] = gather_strip(1, j, rows)
-            s_state[0][j, into, :] = gather_strip(2, j, rows)
-            for i, value in enumerate(look_up(tables, gather_strip(3, j, rows))):
-                s_coef[i, j, into, :] = value
-
+    def strips(blocks):
+        @pl.loop(0, PLANES, unroll=7)
+        def _(j):
+            for k in blocks:
+                rows, into = pl.ds(8 * k, 8), pl.ds(8 + 8 * k, 8)
+                s_field[0][j + 1, into, :] = gather_strip(0, j, rows)
+                s_field[1][j + 1, into, :] = gather_strip(1, j, rows)
+                s_state[0][j, into, :] = gather_strip(2, j, rows)
+                for i, value in enumerate(look_up(tables, gather_strip(3, j, rows))):
+                    s_coef[i, j, into, :] = value
+
+        for k in blocks:
+            rows = pl.ds(8 * k, 8)
+            total = jnp.zeros((8, LANES), F32)
+            for j in range(PLANES):
+                for ref, spare, to in ((r_left, 0, 1), (m_left, 7, 8), (m_right, 0, 65), (r_right, 7, 72)):
+                    value = roll(ref[j, rows, :], to + j - OFFSET[1] - spare)
+                    total = jnp.where((lane == to + j) | (lane == to + j + 48), value, total)
+            s_ghost[pl.ds(8 + 8 * k, 8), :] = total
+
+    receive(0)
+    coefficients((0, 5))
     for k in range(6):
-        rows = pl.ds(8 * k, 8)
-        total = jnp.zeros((8, LANES), F32)
-        for j in range(PLANES):
-            for ref, spare, to in ((r_left, 0, 1), (m_left, 7, 8), (m_right, 0, 65), (r_right, 7, 72)):
-                value = roll(ref[j, rows, :], to + j - OFFSET[1] - spare)
-                total = jnp.where((lane == to + j) | (lane == to + j + 48), value, total)
-        s_ghost[pl.ds(8 + 8 * k, 8), :] = total
+        rows = pl.ds(8 + 8 * k, 8)
+        for plane in (0, NZ + 1):
+            field[1][plane, rows, :] = field[0][plane, rows, :]
+    receive(1)
+    strips((1, 2, 3, 4))
+    receive(2)
+    strips((0, 5))
 
     group = (lane // 16) % 4
 
@@ -348,7 +338,7 @@
 
         main_step(p, q, every, store)
 
-    for copy, dx, dy, _ in transfers:
+    for copy, dx, dy in transfers:
 
         @pl.when(there(dx, dy))
         def _():

time: 32.3 us -> 30.4 us (0.941); the launches traced: 31.8 us -> 30.3 us
  Pallas kernels: 29.7 us -> 28.1 us
    pallas_call x1, Pallas kernels: 29.7 us -> 28.1 us  [body(): pl.pallas_call(lambda *refs: kernel(n_x, n_y, *refs), out_shape=[pltpu.VM...]
where the time goes in v3:
time: 30.4 us; the launch traced here: 30.3 us
  Pallas kernels  28.1 us (92%)
  local copies, waits for them, and re-layouts  1.54 us (5%)
  between operations  0.64 us (2%)
    pallas_call x1, Pallas kernels, body(): pl.pallas_call(lambda *refs: kernel(n_x, n_y, *refs), out_shape=[pltpu.VM...  28.1 us
    unnamed x2, local copies, waits for them, and re-layouts  1.54 us

profile of v3, /device:TPU:22, one launch (start us, length us, event | category | flops | bytes accessed | tf_op | source)
XLA Modules:
  0.0 30.3 jit_solution(341716430857119981)
XLA Ops:
  0.6 28.1 %shard_map.95 = (f32[28,32,128]{2,1,0:T(8,128)S(1)}, f32[28,32,128]{2,1,0:T(8,128)S(1)}) custom-call(f32[28,32,128]{2,1,0:T(8,128)} %refs_0_.1, f32[28,32,128]{2,1,0:T(8,128)} %refs_1_.1, f32[28,32,128]{2,1,0:T(8,128)} %refs_2_.1, s32[28,32,128]{2,1,0:T(8,128)} %refs_3_.1, s32[28,32,128]{2,1,0:T(8,128)} %refs_4_.1, f32[32,128]{1,0:T(8,128)} %refs_5_.1, ...), custom_call_target="tpu_custom_call" | custom-call | tf_op jit(solution)/shard_map/pallas_call | solution.py:374
  28.7 0.8 %copy.12 = f32[28,32,128]{2,1,0:T(8,128)} copy(f32[28,32,128]{2,1,0:T(8,128)S(1)} %get-tuple-element.2) | data formatting | bytes 917504
  29.5 0.8 %copy.13 = f32[28,32,128]{2,1,0:T(8,128)} copy(f32[28,32,128]{2,1,0:T(8,128)S(1)} %get-tuple-element.3) | data formatting | bytes 917504

commit v4 on v3

--- a/solution.py
+++ b/solution.py
@@ -105,6 +105,20 @@
     lane = lane_ids()
     place = lane % 16
     tables = class_tables(table)
+    nothing = jnp.where((lane >= 64) & (place >= 8), float(OUTSIDE), 0.0).astype(F32)
+
+    far = jnp.full((1, LANES), float(OUTSIDE), F32)
+    none = jnp.zeros((1, LANES), F32)
+    for z in range(NZ):
+        for row in (8, 55):
+            cls[z, pl.ds(row, 1), :] = far
+            field[1][z + 1, pl.ds(row, 1), :] = none
+            state[0][z, pl.ds(row, 1), :] = none
+    for ref in (m_left, m_right, r_left, r_right):
+        for j in range(PLANES):
+            for row in (0, TALL - 1):
+                ref[j, pl.ds(row, 1), :] = nothing[0:1]
+
     for load in loads:
         load.wait()
 
@@ -158,15 +172,17 @@
     for dx, message, into in ((1, m_right, r_left), (-1, m_left, r_right)):
         transfer(message.at[:, pl.ds(8, ROWS)], into.at[:, pl.ds(8, ROWS)], dx, 0)
     for dy, main_from, main_to, part_from, part_to in ((1, 40, 8, 32, 0), (-1, 16, 48, 8, 40)):
+        skip = 1 if dy > 0 else 0
+        part_src, part_dst = pl.ds(part_from + skip, 7), pl.ds(part_to + skip, 7)
         for dx, message, into in ((1, m_right, r_left), (-1, m_left, r_right)):
-            transfer(message.at[:, pl.ds(part_from, 8)], into.at[:, pl.ds(part_to, 8)], dx, dy)
-        src, dst = pl.ds(main_from, 8), pl.ds(main_to, 8)
-        transfer(field[0].at[:, src], field[0].at[:, dst], 0, dy)
+            transfer(message.at[:, part_src], into.at[:, part_dst], dx, dy)
+        src, dst = pl.ds(main_from + skip, 7), pl.ds(main_to + skip, 7)
+        transfer(field[0].at[:, pl.ds(main_from, 8)], field[0].at[:, pl.ds(main_to, 8)], 0, dy)
         transfer(field[1].at[pl.ds(1, NZ), src], field[1].at[pl.ds(1, NZ), dst], 0, dy)
         transfer(state[0].at[:, src], state[0].at[:, dst], 0, dy)
         transfer(cls.at[:, src], cls.at[:, dst], 0, dy)
         for message in (m_left, m_right):
-            transfer(message.at[:, pl.ds(part_from, 8)], message.at[:, pl.ds(part_to, 8)], 0, dy)
+            transfer(message.at[:, part_src], message.at[:, part_dst], 0, dy)
 
     for copy, dx, dy in transfers:
 
@@ -174,7 +190,6 @@
         def _():
             copy.start()
 
-    nothing = jnp.where((lane >= 64) & (place >= 8), float(OUTSIDE), 0.0).astype(F32)
 
     def blank(ref, first, rows):
         @pl.loop(0, PLANES)

time: 30.4 us -> 29.8 us (0.980)
  Pallas kernels: 28.1 us -> 27.5 us
    pallas_call x1, Pallas kernels: 28.1 us -> 27.5 us  [body(): pl.pallas_call(lambda *refs: kernel(n_x, n_y, *refs), out_shape=[pltpu.VM...]
where the time goes in v4:
time: 29.8 us; the launch traced here: 29.7 us
  Pallas kernels  27.5 us (92%)
  local copies, waits for them, and re-layouts  1.54 us (5%)
  between operations  0.64 us (2%)
    pallas_call x1, Pallas kernels, body(): pl.pallas_call(lambda *refs: kernel(n_x, n_y, *refs), out_shape=[pltpu.VM...  27.5 us
    unnamed x2, local copies, waits for them, and re-layouts  1.54 us

profile of v4, /device:TPU:22, one launch (start us, length us, event | category | flops | bytes accessed | tf_op | source)
XLA Modules:
  0.0 29.7 jit_solution(15937150858981487878)
XLA Ops:
  0.6 27.5 %shard_map.95 = (f32[28,32,128]{2,1,0:T(8,128)S(1)}, f32[28,32,128]{2,1,0:T(8,128)S(1)}) custom-call(f32[28,32,128]{2,1,0:T(8,128)} %refs_0_.1, f32[28,32,128]{2,1,0:T(8,128)} %refs_1_.1, f32[28,32,128]{2,1,0:T(8,128)} %refs_2_.1, s32[28,32,128]{2,1,0:T(8,128)} %refs_3_.1, s32[28,32,128]{2,1,0:T(8,128)} %refs_4_.1, f32[32,128]{1,0:T(8,128)} %refs_5_.1, ...), custom_call_target="tpu_custom_call" | custom-call | tf_op jit(solution)/shard_map/pallas_call | solution.py:389
  28.1 0.8 %copy.12 = f32[28,32,128]{2,1,0:T(8,128)} copy(f32[28,32,128]{2,1,0:T(8,128)S(1)} %get-tuple-element.2) | data formatting | bytes 917504
  28.9 0.8 %copy.13 = f32[28,32,128]{2,1,0:T(8,128)} copy(f32[28,32,128]{2,1,0:T(8,128)S(1)} %get-tuple-element.3) | data formatting | bytes 917504

commit v5 on v4

--- a/solution.py
+++ b/solution.py
@@ -89,11 +89,11 @@
         pltpu.make_async_copy(src, dst, load_sem.at[i])
         for i, (src, dst) in enumerate(
             [
+                (mask_in, mask),
+                (mat_in, mat),
                 (p_in, field[0].at[pl.ds(1, NZ), own]),
                 (q_in, field[1].at[pl.ds(1, NZ), own]),
                 (v_in, state[0].at[:, own]),
-                (mask_in, mask),
-                (mat_in, mat),
                 (low_in, field[0].at[0, own]),
                 (high_in, field[0].at[NZ + 1, own]),
             ]
@@ -119,7 +119,7 @@
             for row in (0, TALL - 1):
                 ref[j, pl.ds(row, 1), :] = nothing[0:1]
 
-    for load in loads:
+    for load in loads[:2]:
         load.wait()
 
     @pl.loop(0, NZ, unroll=7)
@@ -128,6 +128,9 @@
             rows = pl.ds(8 * k, 8)
             wall = mask[z, rows, :] == 1
             cls[z, pl.ds(16 + 8 * k, 8), :] = jnp.where(wall, mat[z, rows, :], AIR).astype(F32)
+
+    for load in loads[2:]:
+        load.wait()
 
     def merge(bit, low, high):
         return jnp.where((lane & bit) != 0, high, low)

time: 29.8 us -> 29.7 us (level)
  no operation moved by 1% of the time
where the time goes in v5:
time: 29.7 us; the launch traced here: 29.6 us
  Pallas kernels  27.4 us (92%)
  local copies, waits for them, and re-layouts  1.54 us (5%)
  between operations  0.64 us (2%)
    pallas_call x1, Pallas kernels, body(): pl.pallas_call(lambda *refs: kernel(n_x, n_y, *refs), out_shape=[pltpu.VM...  27.4 us
    unnamed x2, local copies, waits for them, and re-layouts  1.54 us

profile of v5, /device:TPU:22, one launch (start us, length us, event | category | flops | bytes accessed | tf_op | source)
XLA Modules:
  0.0 29.6 jit_solution(17232843612185080086)
XLA Ops:
  0.6 27.4 %shard_map.95 = (f32[28,32,128]{2,1,0:T(8,128)S(1)}, f32[28,32,128]{2,1,0:T(8,128)S(1)}) custom-call(f32[28,32,128]{2,1,0:T(8,128)} %refs_0_.1, f32[28,32,128]{2,1,0:T(8,128)} %refs_1_.1, f32[28,32,128]{2,1,0:T(8,128)} %refs_2_.1, s32[28,32,128]{2,1,0:T(8,128)} %refs_3_.1, s32[28,32,128]{2,1,0:T(8,128)} %refs_4_.1, f32[32,128]{1,0:T(8,128)} %refs_5_.1, ...), custom_call_target="tpu_custom_call" | custom-call | tf_op jit(solution)/shard_map/pallas_call | solution.py:392
  28.1 0.8 %copy.12 = f32[28,32,128]{2,1,0:T(8,128)} copy(f32[28,32,128]{2,1,0:T(8,128)S(1)} %get-tuple-element.2) | data formatting | bytes 917504
  28.8 0.8 %copy.13 = f32[28,32,128]{2,1,0:T(8,128)} copy(f32[28,32,128]{2,1,0:T(8,128)S(1)} %get-tuple-element.3) | data formatting | bytes 917504
